TPU v7x, 32 devices: a whole 2x2x4 slice. The times are simulated.
32 devices in a mesh: grp: 16 (over z, y, x), seg: 2 (over core).
Axes of the slice: x: 2, y: 2, z: 4, core: 2. Of those that a mesh axis runs over, the one named last changes fastest.
Arguments:
- queries: bfloat16 [32768, 384], P(('grp', 'seg')), may hold values from -16 to 16
- keys: bfloat16 [32768, 384], P(('grp', 'seg')), may hold values from -16 to 16
- values: bfloat16 [32768, 384], P(('grp', 'seg')), may hold values from -6 to 6
Outputs:
- attended: bfloat16 [32768, 384], P(('grp', 'seg'))
All inputs are finite; a program needn't handle non-finite values.
Results may differ from a plain program's by a relative error of at most 0.0041.
Values may be sent and summed in bfloat16 or wider, within the bound.
A program may use at most 64 MiB of HBM per device.

v0:
```python
import jax
import jax.numpy as jnp
from jax import lax
from jax.sharding import PartitionSpec as P

HEADS = 6
HEAD_WIDTH = 64
SLIDE_GRP = 16


def partner(array, axis, apart):
    return lax.ppermute(array, axis, [(i, i ^ 1 << apart) for i in range(lax.axis_size(axis))])


def attend(query_matrix, key_matrix, value_matrix):
    scores = jnp.einsum(
        "fws,rws->wfr", query_matrix, key_matrix, preferred_element_type=jnp.float32
    ) * HEAD_WIDTH ** (-0.5)
    highest = jnp.max(scores, axis=-1, keepdims=True)
    raised = jnp.exp(scores - highest)
    totals = jnp.sum(raised, axis=-1)
    rounded_length = raised.astype(jnp.bfloat16)
    mixed = (
        jnp.einsum("kgj,jkw->kgw", rounded_length, value_matrix, preferred_element_type=jnp.float32)
        / totals[..., None]
    )
    return (mixed, highest[..., 0] + jnp.log(totals))


def select_rows(source_tensor, period, offsets):
    grouped = source_tensor.reshape(
        source_tensor.shape[0] // period, period, source_tensor.shape[1], source_tensor.shape[2]
    )
    return jnp.stack(
        [grouped[:, offsets[which_head], which_head] for which_head in range(len(offsets))], axis=1
    )


def spread(level_out, level_lse, period, offsets):
    head_total, count, depth = level_out.shape
    marks = (
        jnp.arange(period, dtype=jnp.int32)[None, :] == jnp.array(offsets, dtype=jnp.int32)[:, None]
    )
    cover = jnp.broadcast_to(marks[:, None, :], (head_total, count, period)).reshape(
        head_total, count * period
    )
    out_full = jnp.broadcast_to(
        level_out[:, :, None, :], (head_total, count, period, depth)
    ).reshape(head_total, count * period, depth)
    lse_full = jnp.broadcast_to(level_lse[:, :, None], (head_total, count, period)).reshape(
        head_total, count * period
    )
    return (out_full, lse_full, cover)


def blend(
    near_out,
    near_lse,
    center_output,
    center_logsumexp,
    center_coverage,
    wide_output,
    wide_logsumexp,
    wide_coverage,
):
    mid_level = jnp.where(center_coverage, center_logsumexp, near_lse)
    far_level = jnp.where(wide_coverage, wide_logsumexp, near_lse)
    ceiling = jnp.maximum(jnp.maximum(near_lse, mid_level), far_level)
    near_weight = jnp.exp(near_lse - ceiling)
    mid_weight = jnp.where(center_coverage, jnp.exp(mid_level - ceiling), 0.0)
    far_weight = jnp.where(wide_coverage, jnp.exp(far_level - ceiling), 0.0)
    weighted = (
        near_weight[..., None] * near_out
        + mid_weight[..., None] * center_output
        + far_weight[..., None] * wide_output
    )
    return weighted / (near_weight + mid_weight + far_weight)[..., None]


def body(queries, keys, values):
    row_count = queries.shape[0]
    feature_count = queries.shape[1]
    seg_count = lax.axis_size("seg")
    far_period = SLIDE_GRP * seg_count
    query_split = queries.reshape(row_count, HEADS, HEAD_WIDTH)
    key_split = keys.reshape(row_count, HEADS, HEAD_WIDTH)
    value_split = values.reshape(row_count, HEADS, HEAD_WIDTH)

    def local_head(head_slot):
        start = head_slot * HEAD_WIDTH
        query_cols = lax.dynamic_slice_in_dim(queries, start, HEAD_WIDTH, 1)[:, None, :]
        key_cols = lax.dynamic_slice_in_dim(keys, start, HEAD_WIDTH, 1)[:, None, :]
        value_cols = lax.dynamic_slice_in_dim(values, start, HEAD_WIDTH, 1)[:, None, :]
        mixed, lse_rows = attend(query_cols, key_cols, value_cols)
        return (mixed[0], lse_rows[0])

    near_out, near_lse = lax.map(local_head, jnp.arange(HEADS, dtype=jnp.int32))
    mid_offsets = [which_head % seg_count for which_head in range(HEADS)]
    mid_count = row_count // seg_count
    mid_query = select_rows(query_split, seg_count, mid_offsets)
    mid_key_local = select_rows(key_split, seg_count, mid_offsets).reshape(mid_count, feature_count)
    mid_value_local = select_rows(value_split, seg_count, mid_offsets).reshape(
        mid_count, feature_count
    )
    mid_keys, mid_values = (
        lax.all_gather(mid_key_local, "seg", axis=0, tiled=True),
        lax.all_gather(mid_value_local, "seg", axis=0, tiled=True),
    )
    mid_keys = mid_keys.reshape(row_count, HEADS, HEAD_WIDTH)
    mid_values = mid_values.reshape(row_count, HEADS, HEAD_WIDTH)
    center_output, center_logsumexp = attend(mid_query, mid_keys, mid_values)
    far_offsets = [which_head % far_period for which_head in range(HEADS)]
    far_query = select_rows(query_split, far_period, far_offsets)
    far_key_local = select_rows(key_split, far_period, far_offsets).reshape(-1, feature_count)
    far_value_local = select_rows(value_split, far_period, far_offsets).reshape(-1, feature_count)
    far_keys, far_values = (
        lax.all_gather(far_key_local, "seg", axis=0, tiled=True),
        lax.all_gather(far_value_local, "seg", axis=0, tiled=True),
    )
    grp_place = lax.axis_index("grp")
    for bit in range(SLIDE_GRP.bit_length() - 1):
        other_keys, other_values = partner((far_keys, far_values), "grp", bit)
        upper_half = grp_place // (1 << bit) % 2 == 1
        far_keys = jnp.where(
            upper_half,
            jnp.concatenate([other_keys, far_keys], axis=0),
            jnp.concatenate([far_keys, other_keys], axis=0),
        )
        far_values = jnp.where(
            upper_half,
            jnp.concatenate([other_values, far_values], axis=0),
            jnp.concatenate([far_values, other_values], axis=0),
        )
    wide_output, wide_logsumexp = attend(
        far_query,
        far_keys.reshape(-1, HEADS, HEAD_WIDTH),
        far_values.reshape(-1, HEADS, HEAD_WIDTH),
    )
    center_output_full, center_logsumexp_full, center_coverage = spread(
        center_output, center_logsumexp, seg_count, mid_offsets
    )
    wide_output_full, wide_logsumexp_full, wide_coverage = spread(
        wide_output, wide_logsumexp, far_period, far_offsets
    )
    combined = blend(
        near_out,
        near_lse,
        center_output_full,
        center_logsumexp_full,
        center_coverage,
        wide_output_full,
        wide_logsumexp_full,
        wide_coverage,
    )
    return combined.transpose(1, 0, 2).reshape(row_count, feature_count).astype(jnp.bfloat16)


def solution(mesh):
    return jax.shard_map(
        body,
        mesh=mesh,
        in_specs=(P(("grp", "seg"), None), P(("grp", "seg"), None), P(("grp", "seg"), None)),
        out_specs=P(("grp", "seg"), None),
        check_vma=False,
    )
```

profile of v0, /device:TPU:0, one launch (start us, length us, event | category | flops | bytes accessed | tf_op | source)
XLA Modules:
  0.0 189.8 jit_solution(10579682411492998060)
XLA Ops:
  0.0 2.8 %reshape_reshape.21 = bf16[32,32,6,64]{3,2,1,0:T(8,128)(2,1)S(1)} reshape(bf16[1024,384]{1,0:T(8,128)(2,1)} %param.8) | data formatting | bytes 1572864 | tf_op jit(solution)/shard_map/reshape;reshape | solution.py:31
  3.1 2.1 %all_gather.13 = bf16[64,384]{1,0:T(8,128)(2,1)} all-gather(bf16[32,384]{1,0:T(8,128)(2,1)S(1)} %reshape.178), channel_id=1, replica_groups=mesh['grp'=16,'seg'=2] {'seg'}, dimensions={0}, use_global_device_ids=true | all-gather | bytes 73728 | tf_op jit(solution)/shard_map/all_gather | solution.py:117
  5.2 2.9 %collective-permute-start = (bf16[64,384]{1,0:T(8,128)(2,1)}, bf16[64,384]{1,0:T(8,128)(2,1)}, u32[]{:S(2)}, u32[]{:S(2)}) collective-permute-start(bf16[64,384]{1,0:T(8,128)(2,1)} %all_gather.13), channel_id=1, source_target_pairs={{0,2},{2,0},{4,6},{6,4},{8,10},{10,8},{12,14},{14,12},{16,18},{18,... | collective-permute-start | bytes 147464 | tf_op jit(solution)/shard_map/ppermute | solution.py:12
  8.1 2.1 %reshape_reshape.23 = bf16[32,32,6,64]{3,2,1,0:T(8,128)(2,1)} reshape(bf16[1024,384]{1,0:T(8,128)(2,1)S(1)} %copy-done.3) | data formatting | bytes 1572864 | tf_op jit(solution)/shard_map/reshape;reshape | solution.py:31
  11.6 2.0 %all_gather.15 = bf16[64,384]{1,0:T(8,128)(2,1)} all-gather(bf16[32,384]{1,0:T(8,128)(2,1)S(1)} %reshape.183), channel_id=1, replica_groups=mesh['grp'=16,'seg'=2] {'seg'}, dimensions={0}, use_global_device_ids=true | all-gather | bytes 73728 | tf_op jit(solution)/shard_map/all_gather | solution.py:118
  13.6 2.1 %reshape_reshape.22 = bf16[512,2,6,64]{3,2,1,0:T(8,128)(2,1)} reshape(bf16[1024,384]{1,0:T(8,128)(2,1)S(1)} %copy-done.3) | data formatting | bytes 1572864 | tf_op jit(solution)/shard_map/reshape;reshape | solution.py:31
  15.8 2.1 %reshape_reshape.19 = bf16[512,2,6,64]{3,2,1,0:T(8,128)(2,1)} reshape(bf16[1024,384]{1,0:T(8,128)(2,1)S(1)} %copy-done.1) | data formatting | bytes 1572864 | tf_op jit(solution)/shard_map/reshape;reshape | solution.py:31
  17.9 2.2 %reshape_reshape.18 = bf16[512,2,6,64]{3,2,1,0:T(8,128)(2,1)} reshape(bf16[1024,384]{1,0:T(8,128)(2,1)S(1)} %copy-done) | data formatting | bytes 1572864 | tf_op jit(solution)/shard_map/reshape;reshape | solution.py:31
  20.1 2.1 %reshape_reshape.20 = bf16[32,32,6,64]{3,2,1,0:T(8,128)(2,1)} reshape(bf16[1024,384]{1,0:T(8,128)(2,1)S(1)} %copy-done) | data formatting | bytes 1572864 | tf_op jit(solution)/shard_map/reshape;reshape | solution.py:31
  22.2 4.7 %fusion.54 = (bf16[512,1,1,64]{3,2,1,0:T(2,128)(2,1)S(1)}, bf16[512,1,1,64]{3,2,1,0:T(2,128)(2,1)S(1)}, bf16[512,1,1,64]{3,2,1,0:T(2,128)(2,1)S(1)}, bf16[512,1,...) fusion(bf16[512,2,6,64]{3,2,1,0:T(8,128)(2,1)} %reshape_reshape.22), kind=kLoop, calls=%fused_computation.117 | loop fusion | bytes 786432 | tf_op jit(solution)/shard_map/slice | solution.py:35
  27.7 2.5 %all_gather.14 = bf16[1024,384]{0,1:T(8,128)(2,1)} all-gather(bf16[512,384]{0,1:T(8,128)(2,1)S(1)} %bitcast.137), channel_id=1, replica_groups=mesh['grp'=16,'seg'=2] {'seg'}, dimensions={0}, use_global_device_ids=true | all-gather | bytes 1179648 | tf_op jit(solution)/shard_map/all_gather | solution.py:107
  30.2 4.8 %fusion.53 = (bf16[512,1,1,64]{3,2,1,0:T(2,128)(2,1)S(1)}, bf16[512,1,1,64]{3,2,1,0:T(2,128)(2,1)S(1)}, bf16[512,1,1,64]{3,2,1,0:T(2,128)(2,1)S(1)}, bf16[512,1,...) fusion(bf16[512,2,6,64]{3,2,1,0:T(8,128)(2,1)} %reshape_reshape.18), kind=kLoop, calls=%fused_computation.116 | loop fusion | bytes 786432 | tf_op jit(solution)/shard_map/slice | solution.py:35
  38.9 4.7 %fusion.52 = (bf16[512,1,1,64]{3,2,1,0:T(2,128)(2,1)S(1)}, bf16[512,1,1,64]{3,2,1,0:T(2,128)(2,1)S(1)}, bf16[512,1,1,64]{3,2,1,0:T(2,128)(2,1)S(1)}, bf16[512,1,...) fusion(bf16[512,2,6,64]{3,2,1,0:T(8,128)(2,1)} %reshape_reshape.19), kind=kLoop, calls=%fused_computation.115 | loop fusion | bytes 786432 | tf_op jit(solution)/shard_map/slice | solution.py:35
  47.3 2.4 %all_gather.12 = bf16[1024,384]{0,1:T(8,128)(2,1)S(1)} all-gather(bf16[512,384]{0,1:T(8,128)(2,1)S(1)} %bitcast.138), channel_id=1, replica_groups=mesh['grp'=16,'seg'=2] {'seg'}, dimensions={0}, use_global_device_ids=true | all-gather | bytes 1179648 | tf_op jit(solution)/shard_map/all_gather | solution.py:106
  53.0 2.9 %multiply_reduce_fusion.1 = (f32[6,512]{1,0:T(8,128)S(1)}, f32[6,512,1024]{2,1,0:T(8,128)S(1)}) fusion(bf16[512,6,64]{0,2,1:T(8,128)(2,1)} %copy-done.7, bf16[1024,6,64]{0,2,1:T(8,128)(2,1)S(1)} %bitcast.132), kind=kOutput, calls=%fused_computation.17 | convolution fusion | flops 408941568 | bytes 13774848 | tf_op jit(solution)/shard_map/fws,rws->wfr/dot_general | solution.py:16
  55.9 2.8 %fusion.21 = f32[6,512]{1,0:T(8,128)S(1)} fusion(f32[6,512,1024]{2,1,0:T(8,128)S(1)} %get-tuple-element.102, f32[6,512]{1,0:T(8,128)S(1)} %get-tuple-element.101), kind=kLoop, calls=%fused_computation.19 | loop fusion | flops 9434112 | bytes 12607488 | tf_op jit(solution)/shard_map/reduce_sum | solution.py:21
  58.7 4.5 %fusion.27 = f32[6,512,64]{1,2,0:T(8,128)} fusion(bf16[1024,6,64]{0,2,1:T(8,128)(2,1)} %bitcast.134, f32[6,512,1024]{2,1,0:T(8,128)S(1)} %get-tuple-element.102, f32[6,512]{1,0:T(8,128)S(1)} %get-tuple-element.101, f32[6,512]{1,0:T(8,128)S(1)} %fusion.21), kind=kOutput, calls=%fused_computation.27 | convolution fusion | flops 412286976 | bytes 14180352 | tf_op jit(solution)/shard_map/kgj,jkw->kgw/dot_general | solution.py:24
  63.2 40.4 %while.13 = (s32[]{:T(128)}, f32[6,1024,64]{1,2,0:T(8,128)}, f32[6,1024]{1,0:T(8,128)}, s32[6]{0:T(128)S(1)}, bf16[1024,384]{1,0:T(8,128)(2,1)S(1)}, /*index=5*/...) while((s32[]{:T(128)}, f32[6,1024,64]{1,2,0:T(8,128)}, f32[6,1024]{1,0:T(8,128)}, ...), condition=%wide.region_3.4_spmd.clone, body=%wide.region_0.3_spmd.sunk.clone | while | flops 276888576 | bytes 13673635 | solution.py:97
  66.0 2.6 %fusion.71 = f32[6,1024,64]{1,2,0:T(8,128)} fusion(f32[6,1024,64]{1,2,0:T(8,128)} %get-tuple-element.186, s32[]{:T(128)S(6)} %copy.438, f32[1024,1024]{0,1:T(8,128)S(1)} %get-tuple-element.163, f32[1024]{0:T(1024)S(1)} %get-tuple-element.164, bf16[1024,384]{1,0:T(8,128)(2,1)} %get-tuple-element.199, s32[]{:T(128)S(6)} %select_n.218, ...), kind=kOutput, calls=%fused_computation.7.clone.1.clone | convolution fusion | flops 137428992 | bytes 4726792 | tf_op jit(solution)/shard_map/while/body/eval_jaxpr/kgj,jkw->kgw/dot_general | solution.py:24
  72.7 2.6 %fusion.71 = f32[6,1024,64]{1,2,0:T(8,128)} fusion(f32[6,1024,64]{1,2,0:T(8,128)} %get-tuple-element.186, s32[]{:T(128)S(6)} %copy.438, f32[1024,1024]{0,1:T(8,128)S(1)} %get-tuple-element.163, f32[1024]{0:T(1024)S(1)} %get-tuple-element.164, bf16[1024,384]{1,0:T(8,128)(2,1)} %get-tuple-element.199, s32[]{:T(128)S(6)} %select_n.218, ...), kind=kOutput, calls=%fused_computation.7.clone.1.clone | convolution fusion | flops 137428992 | bytes 4726792 | tf_op jit(solution)/shard_map/while/body/eval_jaxpr/kgj,jkw->kgw/dot_general | solution.py:24
  79.5 2.6 %fusion.71 = f32[6,1024,64]{1,2,0:T(8,128)} fusion(f32[6,1024,64]{1,2,0:T(8,128)} %get-tuple-element.186, s32[]{:T(128)S(6)} %copy.438, f32[1024,1024]{0,1:T(8,128)S(1)} %get-tuple-element.163, f32[1024]{0:T(1024)S(1)} %get-tuple-element.164, bf16[1024,384]{1,0:T(8,128)(2,1)} %get-tuple-element.199, s32[]{:T(128)S(6)} %select_n.218, ...), kind=kOutput, calls=%fused_computation.7.clone.1.clone | convolution fusion | flops 137428992 | bytes 4726792 | tf_op jit(solution)/shard_map/while/body/eval_jaxpr/kgj,jkw->kgw/dot_general | solution.py:24
  86.2 2.5 %fusion.71 = f32[6,1024,64]{1,2,0:T(8,128)} fusion(f32[6,1024,64]{1,2,0:T(8,128)} %get-tuple-element.186, s32[]{:T(128)S(6)} %copy.438, f32[1024,1024]{0,1:T(8,128)S(1)} %get-tuple-element.163, f32[1024]{0:T(1024)S(1)} %get-tuple-element.164, bf16[1024,384]{1,0:T(8,128)(2,1)} %get-tuple-element.199, s32[]{:T(128)S(6)} %select_n.218, ...), kind=kOutput, calls=%fused_computation.7.clone.1.clone | convolution fusion | flops 137428992 | bytes 4726792 | tf_op jit(solution)/shard_map/while/body/eval_jaxpr/kgj,jkw->kgw/dot_general | solution.py:24
  92.9 2.6 %fusion.71 = f32[6,1024,64]{1,2,0:T(8,128)} fusion(f32[6,1024,64]{1,2,0:T(8,128)} %get-tuple-element.186, s32[]{:T(128)S(6)} %copy.438, f32[1024,1024]{0,1:T(8,128)S(1)} %get-tuple-element.163, f32[1024]{0:T(1024)S(1)} %get-tuple-element.164, bf16[1024,384]{1,0:T(8,128)(2,1)} %get-tuple-element.199, s32[]{:T(128)S(6)} %select_n.218, ...), kind=kOutput, calls=%fused_computation.7.clone.1.clone | convolution fusion | flops 137428992 | bytes 4726792 | tf_op jit(solution)/shard_map/while/body/eval_jaxpr/kgj,jkw->kgw/dot_general | solution.py:24
  99.7 2.5 %fusion.71 = f32[6,1024,64]{1,2,0:T(8,128)} fusion(f32[6,1024,64]{1,2,0:T(8,128)} %get-tuple-element.186, s32[]{:T(128)S(6)} %copy.438, f32[1024,1024]{0,1:T(8,128)S(1)} %get-tuple-element.163, f32[1024]{0:T(1024)S(1)} %get-tuple-element.164, bf16[1024,384]{1,0:T(8,128)(2,1)} %get-tuple-element.199, s32[]{:T(128)S(6)} %select_n.218, ...), kind=kOutput, calls=%fused_computation.7.clone.1.clone | convolution fusion | flops 137428992 | bytes 4726792 | tf_op jit(solution)/shard_map/while/body/eval_jaxpr/kgj,jkw->kgw/dot_general | solution.py:24
  110.8 2.1 %copy.342 = f32[6,1024,64]{2,1,0:T(8,128)S(1)} copy(f32[6,1024,64]{1,2,0:T(8,128)} %get-tuple-element.44) | data formatting | bytes 3145728 | tf_op jit(solution)/shard_map/while | solution.py:97
  120.5 2.1 %collective-permute-start.1 = (bf16[128,384]{1,0:T(8,128)(2,1)S(1)}, bf16[128,384]{1,0:T(8,128)(2,1)S(1)}, u32[]{:S(2)}, u32[]{:S(2)}) collective-permute-start(bf16[128,384]{1,0:T(8,128)(2,1)S(1)} %maximum_select_fusion.12), channel_id=1, source_target_pairs={{0,4},{2,6},{4,0},{6,2},{8,12},{10,14},{12,8},{14,10},{16,20},{18,... | collective-permute-start | bytes 294920 | tf_op jit(solution)/shard_map/ppermute | solution.py:12
  126.7 2.1 %maximum_select_fusion.13 = (bf16[128,6,64]{0,2,1:T(8,128)(2,1)}, bf16[128,6,64]{0,2,1:T(8,128)(2,1)}) fusion(bf16[64,6,64]{0,2,1:T(8,128)(2,1)} %bitcast.144, bf16[64,6,64]{0,2,1:T(8,128)(2,1)} %bitcast.146, pred[]{:T(512)S(6)} %eq.60, bf16[64,6,64]{0,2,1:T(8,128)(2,1)} %bitcast.147, bf16[64,6,64]{0,2,1:T(8,128)(2,1)} %bitcast.145), kind=kLoop, calls=%fused_computation.55 | loop fusion | flops 884736 | bytes 393217 | tf_op jit(solution)/shard_map/jit(_where)/select_n | solution.py:124
  130.2 2.1 %collective-permute-start.2 = (bf16[256,384]{1,0:T(8,128)(2,1)}, bf16[256,384]{1,0:T(8,128)(2,1)S(1)}, u32[]{:S(2)}, u32[]{:S(2)}) collective-permute-start(bf16[256,384]{1,0:T(8,128)(2,1)} %maximum_select_fusion.8), channel_id=1, source_target_pairs={{0,8},{2,10},{4,12},{6,14},{8,0},{10,2},{12,4},{14,6},{16,24},{18,... | collective-permute-start | bytes 589832 | tf_op jit(solution)/shard_map/ppermute | solution.py:12
  140.5 3.0 %collective-permute-start.3 = (bf16[512,384]{1,0:T(8,128)(2,1)}, bf16[512,384]{1,0:T(8,128)(2,1)}, u32[]{:S(2)}, u32[]{:S(2)}) collective-permute-start(bf16[512,384]{1,0:T(8,128)(2,1)} %maximum_select_fusion.4), channel_id=1, source_target_pairs={{0,16},{2,18},{4,20},{6,22},{8,24},{10,26},{12,28},{14,30},{16,0},... | collective-permute-start | bytes 1179656 | tf_op jit(solution)/shard_map/ppermute | solution.py:12
  148.2 2.1 %maximum_select_fusion.5 = bf16[512,6,64]{0,2,1:T(8,128)(2,1)} fusion(bf16[256,6,64]{0,2,1:T(8,128)(2,1)} %maximum_select_fusion.9, bf16[256,6,64]{0,2,1:T(8,128)(2,1)} %bitcast.136, pred[]{:T(512)S(6)} %eq.58), kind=kLoop, calls=%fused_computation.46 | loop fusion | flops 1769472 | bytes 786433 | tf_op jit(solution)/shard_map/jit(_where)/select_n | solution.py:124
  152.2 18.1 %collective-permute-done.3 = bf16[512,384]{1,0:T(8,128)(2,1)} collective-permute-done((bf16[512,384]{1,0:T(8,128)(2,1)}, bf16[512,384]{1,0:T(8,128)(2,1)}, u32[]{:S(2)}, u32[]{:S(2)}) %collective-permute-start.3) | collective-permute-done | bytes 393248 | tf_op jit(solution)/shard_map/ppermute | solution.py:12
  181.8 5.2 %fusion.26 = bf16[6,1024,64]{2,1,0:T(8,128)(2,1)} fusion(f32[6,1024,64]{2,1,0:T(8,128)S(1)} %bitcast.129, f32[6,1024,64]{2,1,0:T(8,128)S(1)} %copy.342, f32[6,1024]{1,0:T(8,128)S(1)} %get-tuple-element.59, f32[6,32,64]{2,1,0:T(8,128)S(1)} %convolution_divide_fusion, f32[6,1024]{1,0:T(8,128)S(1)} %get-tuple-element.62, f32[6,1024]{1,0:T(8,128)S(1)} %get-tuple-element.60, ...), kind=kLoop, calls=%fused_computation.24 | loop fusion | flops 2752512 | bytes 4079616 | tf_op jit(solution)/shard_map/convert_element_type | solution.py:155
  (185 shorter events, 83.5 us)
Async XLA Ops:
  0.0 8.1 %copy-start.3 = (bf16[1024,384]{1,0:T(8,128)(2,1)S(1)}, bf16[1024,384]{1,0:T(8,128)(2,1)}, u32[]{:S(2)}) copy-start(bf16[1024,384]{1,0:T(8,128)(2,1)} %param.9) | copy-start | bytes 2359300
  5.2 10.6 %copy-start.1 = (bf16[1024,384]{1,0:T(8,128)(2,1)S(1)}, bf16[1024,384]{1,0:T(8,128)(2,1)}, u32[]{:S(2)}) copy-start(bf16[1024,384]{1,0:T(8,128)(2,1)} %param.8) | copy-start | bytes 2359300
  5.2 114.4 %collective-permute-start = (bf16[64,384]{1,0:T(8,128)(2,1)}, bf16[64,384]{1,0:T(8,128)(2,1)}, u32[]{:S(2)}, u32[]{:S(2)}) collective-permute-start(bf16[64,384]{1,0:T(8,128)(2,1)} %all_gather.13), channel_id=1, source_target_pairs={{0,2},{2,0},{4,6},{6,4},{8,10},{10,8},{12,14},{14,12},{16,18},{18,... | collective-permute-start | bytes 147464 | tf_op jit(solution)/shard_map/ppermute | solution.py:12
  11.3 6.6 %copy-start = (bf16[1024,384]{1,0:T(8,128)(2,1)S(1)}, bf16[1024,384]{1,0:T(8,128)(2,1)}, u32[]{:S(2)}) copy-start(bf16[1024,384]{1,0:T(8,128)(2,1)} %param.7) | copy-start | bytes 2359300
  13.5 109.1 %collective-permute-start.4 = (bf16[64,384]{1,0:T(8,128)(2,1)}, bf16[64,384]{1,0:T(8,128)(2,1)}, u32[]{:S(2)}, u32[]{:S(2)}) collective-permute-start(bf16[64,384]{1,0:T(8,128)(2,1)} %all_gather.15), channel_id=1, source_target_pairs={{0,2},{2,0},{4,6},{6,4},{8,10},{10,8},{12,14},{14,12},{16,18},{18,... | collective-permute-start | bytes 147464 | tf_op jit(solution)/shard_map/ppermute | solution.py:12
  44.5 5.2 %copy-start.6 = (bf16[512,6,64]{0,2,1:T(8,128)(2,1)S(1)}, bf16[512,6,64]{0,2,1:T(8,128)(2,1)}, u32[]{:S(2)}) copy-start(bf16[512,6,64]{0,2,1:T(8,128)(2,1)} %constant_dynamic-update-slice_fusion.5) | copy-start | bytes 1179652
  45.2 7.0 %copy-start.10 = (bf16[512,1,1,64]{0,3,2,1:T(8,128)(2,1)S(1)}, bf16[512,1,1,64]{0,3,2,1:T(8,128)(2,1)}, u32[]{:S(2)}) copy-start(bf16[512,1,1,64]{0,3,2,1:T(8,128)(2,1)} %copy.381) | copy-start | bytes 196612
  52.2 0.7 copy-start.7
  63.2 40.4 %copy-start.19 = (s32[6]{0:T(128)S(1)}, s32[6]{0:T(128)}, u32[]{:S(2)}) copy-start(s32[6]{0:T(128)} %constant.106.clone) | copy-start | bytes 76
  63.2 45.9 %copy-start.5 = (f32[6,512,64]{1,2,0:T(8,128)S(1)}, f32[6,512,64]{1,2,0:T(8,128)}, u32[]{:S(2)}) copy-start(f32[6,512,64]{1,2,0:T(8,128)} %fusion.27) | copy-start | bytes 2359300
  105.5 5.3 %copy-start.18 = (bf16[32,6,64]{2,0,1:T(8,128)(2,1)}, bf16[32,6,64]{2,0,1:T(8,128)(2,1)S(1)}, u32[]{:S(2)}) copy-start(bf16[32,6,64]{2,0,1:T(8,128)(2,1)S(1)} %constant_dynamic-update-slice_fusion.12) | copy-start | bytes 73732
  120.5 8.3 %collective-permute-start.1 = (bf16[128,384]{1,0:T(8,128)(2,1)S(1)}, bf16[128,384]{1,0:T(8,128)(2,1)S(1)}, u32[]{:S(2)}, u32[]{:S(2)}) collective-permute-start(bf16[128,384]{1,0:T(8,128)(2,1)S(1)} %maximum_select_fusion.12), channel_id=1, source_target_pairs={{0,4},{2,6},{4,0},{6,2},{8,12},{10,14},{12,8},{14,10},{16,20},{18,... | collective-permute-start | bytes 294920 | tf_op jit(solution)/shard_map/ppermute | solution.py:12
  123.5 8.7 %collective-permute-start.5 = (bf16[128,384]{1,0:T(8,128)(2,1)S(1)}, bf16[128,384]{1,0:T(8,128)(2,1)S(1)}, u32[]{:S(2)}, u32[]{:S(2)}) collective-permute-start(bf16[128,384]{1,0:T(8,128)(2,1)S(1)} %maximum_select_fusion.14), channel_id=1, source_target_pairs={{0,4},{2,6},{4,0},{6,2},{8,12},{10,14},{12,8},{14,10},{16,20},{18,... | collective-permute-start | bytes 294920 | tf_op jit(solution)/shard_map/ppermute | solution.py:12
  128.8 0.6 copy-start.8
  130.2 8.5 %collective-permute-start.2 = (bf16[256,384]{1,0:T(8,128)(2,1)}, bf16[256,384]{1,0:T(8,128)(2,1)S(1)}, u32[]{:S(2)}, u32[]{:S(2)}) collective-permute-start(bf16[256,384]{1,0:T(8,128)(2,1)} %maximum_select_fusion.8), channel_id=1, source_target_pairs={{0,8},{2,10},{4,12},{6,14},{8,0},{10,2},{12,4},{14,6},{16,24},{18,... | collective-permute-start | bytes 589832 | tf_op jit(solution)/shard_map/ppermute | solution.py:12
  132.3 0.6 copy-start.9
  133.6 11.8 %collective-permute-start.6 = (bf16[256,384]{1,0:T(8,128)(2,1)}, bf16[256,384]{1,0:T(8,128)(2,1)S(1)}, u32[]{:S(2)}, u32[]{:S(2)}) collective-permute-start(bf16[256,384]{1,0:T(8,128)(2,1)} %maximum_select_fusion.10), channel_id=1, source_target_pairs={{0,8},{2,10},{4,12},{6,14},{8,0},{10,2},{12,4},{14,6},{16,24},{18,... | collective-permute-start | bytes 589832 | tf_op jit(solution)/shard_map/ppermute | solution.py:12
  140.5 29.7 %collective-permute-start.3 = (bf16[512,384]{1,0:T(8,128)(2,1)}, bf16[512,384]{1,0:T(8,128)(2,1)}, u32[]{:S(2)}, u32[]{:S(2)}) collective-permute-start(bf16[512,384]{1,0:T(8,128)(2,1)} %maximum_select_fusion.4), channel_id=1, source_target_pairs={{0,16},{2,18},{4,20},{6,22},{8,24},{10,26},{12,28},{14,30},{16,0},... | collective-permute-start | bytes 1179656 | tf_op jit(solution)/shard_map/ppermute | solution.py:12
  147.3 30.2 %collective-permute-start.7 = (bf16[512,384]{1,0:T(8,128)(2,1)}, bf16[512,384]{1,0:T(8,128)(2,1)}, u32[]{:S(2)}, u32[]{:S(2)}) collective-permute-start(bf16[512,384]{1,0:T(8,128)(2,1)} %maximum_select_fusion.6), channel_id=1, source_target_pairs={{0,16},{2,18},{4,20},{6,22},{8,24},{10,26},{12,28},{14,30},{16,0},... | collective-permute-start | bytes 1179656 | tf_op jit(solution)/shard_map/ppermute | solution.py:12
  173.0 0.9 copy-start.4
  173.0 1.2 copy-start.16
  173.0 7.6 %copy-start.14 = (pred[6,1024]{1,0:T(8,128)(4,1)S(1)}, pred[6,1024]{1,0:T(8,128)(4,1)}, u32[]{:S(2)}) copy-start(pred[6,1024]{1,0:T(8,128)(4,1)} %reshape.173) | copy-start | bytes 18436
  173.0 7.6 %copy-start.15 = (pred[6,1024]{1,0:T(8,128)(4,1)S(1)}, pred[6,1024]{1,0:T(8,128)(4,1)}, u32[]{:S(2)}) copy-start(pred[6,1024]{1,0:T(8,128)(4,1)} %reshape.177) | copy-start | bytes 18436
  174.1 0.6 copy-start.17
  178.6 2.0 %copy-start.11 = (f32[6,1024]{1,0:T(8,128)S(1)}, f32[6,1024]{1,0:T(8,128)}, u32[]{:S(2)}) copy-start(f32[6,1024]{1,0:T(8,128)} %copy.327) | copy-start | bytes 73732
  178.7 2.0 %copy-start.12 = (f32[6,1024]{1,0:T(8,128)S(1)}, f32[6,1024]{1,0:T(8,128)}, u32[]{:S(2)}) copy-start(f32[6,1024]{1,0:T(8,128)} %reshape.179) | copy-start | bytes 73732
  178.7 2.0 %copy-start.13 = (f32[6,1024]{1,0:T(8,128)S(1)}, f32[6,1024]{1,0:T(8,128)}, u32[]{:S(2)}) copy-start(f32[6,1024]{1,0:T(8,128)} %get-tuple-element.43) | copy-start | bytes 73732
  178.7 2.0 %copy-start.2 = (f32[6,512,64]{2,1,0:T(8,128)S(1)}, f32[6,512,64]{2,1,0:T(8,128)}, u32[]{:S(2)}) copy-start(f32[6,512,64]{2,1,0:T(8,128)} %copy.349) | copy-start | bytes 2359300
where the time goes:
time: 192 us; the launch traced here: 190 us
  local copies, waits for them, and re-layouts  84.6 us (44%)
  matrix products  31 us (16%)
  other arithmetic  30.6 us (16%)
  waiting for transfers between devices  20.1 us (10%)
  starting transfers between devices  10.2 us (5%)
  blocking collectives  8.92 us (5%)
  loops' own time  3.86 us (2%)
    dot_general x8, matrix products, attend(): jnp.einsum('kgj,jkw->kgw', rounded_length, value_matrix, preferred_elemen...  21.8 us
    ppermute x8, waiting for transfers between devices, partner(): lax.ppermute(array, axis, [(i, i ^ 1 << apart) for i in range(lax.axis_si...  20.1 us
    slice x18, local copies, waits for them, and re-layouts, select_rows(): grouped[:, offsets[which_head], which_head]  19.1 us
    another operation x6, local copies, waits for them, and re-layouts, select_rows(): source_tensor.reshape(source_tensor.shape[0] // period, period, source_te...  13.4 us
    unnamed x76, local copies, waits for them, and re-layouts  11.8 us
    ppermute x8, starting transfers between devices, partner(): lax.ppermute(array, axis, [(i, i ^ 1 << apart) for i in range(lax.axis_si...  10.2 us
    select_n x6, other arithmetic, body(): jnp.where(upper_half, jnp.concatenate([other_keys, far_keys], axis=0), jn...  9.45 us
    dot_general x8, matrix products, attend(): jnp.einsum('fws,rws->wfr', query_matrix, key_matrix, preferred_element_ty...  9.24 us
  transfers between devices with their start and end apart: 8, of which 2 were waited for; matrix products, arithmetic and copies ran while one was open for 67% of the time, Pallas kernels for 0%

commit v1 on v0

v1 whole, which is shorter than its diff:
```python
import functools

import jax
import jax.numpy as jnp
from jax import lax
from jax.experimental import pallas as pl
from jax.experimental.pallas import tpu as pltpu
from jax.sharding import PartitionSpec as P

HEAD_WIDTH = 64
PAIR = 2 * HEAD_WIDTH
SLIDE_GRP = 16
BLOCK = 256

MESH = pl.DeviceIdType.MESH
F32 = jnp.float32
BF16 = jnp.bfloat16


def scores_of(query, key):
    return lax.dot_general(query, key, (((1,), (1,)), ((), ())), preferred_element_type=F32)


def attend(query, keys, values):
    scores = [scores_of(query, key) for key in keys]
    highest = functools.reduce(
        jnp.maximum, [jnp.max(one, axis=-1, keepdims=True) for one in scores]
    )
    total = None
    for one, value in zip(scores, values):
        raised = jnp.exp(one - highest).astype(BF16)
        part = jnp.dot(raised, value, preferred_element_type=F32)
        total = part if total is None else total + part
    return total, highest


def divide(total):
    return total / pltpu.roll(total, HEAD_WIDTH, 1)


def kernel(
    seg_count,
    q_ref, k_ref, v_ref, o_ref,
    q32, k32, v32, qm, kp, va, vb, mid_out, mid_in, vmid, far, outp, acc_s, max_s,
    mid_send, mid_recv, far_send, far_recv, fwd_send, fwd_recv,
):
    rows = q_ref.shape[0]
    pairs = q_ref.shape[1] // PAIR
    mid = rows // seg_count
    period = SLIDE_GRP * seg_count
    far_rows = rows // period
    far_pad = far.shape[4]
    block = min(BLOCK, mid)
    grp, seg = lax.axis_index("grp"), lax.axis_index("seg")
    place = lax.rem(grp, SLIDE_GRP)
    base = grp - place

    barrier = pltpu.get_barrier_semaphore()
    for step in range(1, SLIDE_GRP):
        peer = base + lax.rem(place + step, SLIDE_GRP)
        pl.semaphore_signal(barrier, inc=1, device_id=(peer, seg), device_id_type=MESH)
    for step in range(1, seg_count):
        peer = lax.rem(seg + step, seg_count)
        pl.semaphore_signal(barrier, inc=1, device_id=(grp, peer), device_id_type=MESH)

    def left_of(count):
        return lax.broadcasted_iota(jnp.int32, (count, PAIR), 1) < HEAD_WIDTH

    left = left_of(mid)
    far_left = left_of(far_rows)

    def far_slot(array, pair):
        picked = jnp.where(
            far_left,
            array[pair, pl.ds((2 * pair) % period, far_rows, stride=period), :],
            array[pair, pl.ds((2 * pair + 1) % period, far_rows, stride=period), :],
        )
        if far_pad > far_rows:
            picked = jnp.concatenate([picked] * (far_pad // far_rows), axis=0)
        return picked.astype(BF16)

    for pair in range(pairs):
        columns = slice(pair * PAIR, (pair + 1) * PAIR)
        even, odd = (2 * pair) % seg_count, (2 * pair + 1) % seg_count
        k32[pair] = k_ref[:, columns].astype(F32)
        v32[pair] = v_ref[:, columns].astype(F32)
        mid_out[0, pair] = jnp.where(
            left,
            k32[pair, pl.ds(even, mid, stride=seg_count), :],
            k32[pair, pl.ds(odd, mid, stride=seg_count), :],
        ).astype(BF16)
        mid_out[1, pair] = jnp.where(
            left,
            v32[pair, pl.ds(even, mid, stride=seg_count), :],
            v32[pair, pl.ds(odd, mid, stride=seg_count), :],
        ).astype(BF16)
        far[seg, place, 0, pair] = far_slot(k32, pair)
        far[seg, place, 1, pair] = far_slot(v32, pair)

    pl.semaphore_wait(barrier, SLIDE_GRP - 1 + seg_count - 1)

    mid_copies = []
    for step in range(1, seg_count):
        peer = lax.rem(seg + step, seg_count)
        copy = pltpu.make_async_remote_copy(
            src_ref=mid_out,
            dst_ref=mid_in.at[seg_count - 1 - step],
            send_sem=mid_send.at[step - 1],
            recv_sem=mid_recv.at[seg_count - 1 - step],
            device_id=(grp, peer),
            device_id_type=MESH,
        )
        copy.start()
        mid_copies.append(copy)
    far_copies = []
    for step in range(1, SLIDE_GRP):
        peer = base + lax.rem(place + step, SLIDE_GRP)
        copy = pltpu.make_async_remote_copy(
            src_ref=far.at[seg, place],
            dst_ref=far.at[seg, place],
            send_sem=far_send.at[step - 1],
            recv_sem=far_recv.at[SLIDE_GRP - 1 - step],
            device_id=(peer, seg),
            device_id_type=MESH,
        )
        copy.start()
        far_copies.append(copy)

    for pair in range(pairs):
        columns = slice(pair * PAIR, (pair + 1) * PAIR)
        q32[pair] = q_ref[:, columns].astype(F32) * HEAD_WIDTH ** (-0.5)
        for residue in range(seg_count):
            target = pl.ds(residue * mid, mid)
            source = pl.ds(residue, mid, stride=seg_count)
            query = q32[pair, source, :]
            qm[2 * pair, target] = jnp.where(left, query, 0.0).astype(BF16)
            qm[2 * pair + 1, target] = jnp.where(left, 0.0, query).astype(BF16)
            kp[pair, target] = k32[pair, source, :].astype(BF16)
            value = v32[pair, source, :]
            for side in range(2):
                head = 2 * pair + side
                full = jnp.where(left, value, 1.0) if side == 0 else jnp.where(left, 1.0, value)
                va[head, target] = full.astype(BF16)
                if residue == head % seg_count:
                    full = full * 2.0
                vb[head, target] = full.astype(BF16)

    def lanes(side):
        return slice(side * HEAD_WIDTH, (side + 1) * HEAD_WIDTH)

    outer_blocks = (rows - mid) // block

    def outer(index, carry):
        pair = index // outer_blocks
        part = index % outer_blocks
        for side in range(2):
            head = 2 * pair + side
            own = head % seg_count
            start = ((own + 1) * mid + part * block) % rows
            target = pl.ds(pl.multiple_of(start, block), block)
            total, _ = attend(qm[head, target], [kp[pair]], [va[head]])
            outp[pair, target, lanes(side)] = divide(total)[:, lanes(side)]
        return carry

    lax.fori_loop(0, pairs * outer_blocks, outer, 0)

    for copy in mid_copies:
        copy.wait()
    away = (seg_count - 1) * mid
    away_left = left_of(away)
    for pair in range(pairs):
        value = mid_in[:, 1, pair].reshape(away, PAIR).astype(F32)
        vmid[2 * pair] = jnp.where(away_left, value, 1.0).astype(BF16)
        vmid[2 * pair + 1] = jnp.where(away_left, 1.0, value).astype(BF16)

    inner_blocks = mid // block

    def inner(index, carry):
        pair = index // inner_blocks
        part = index % inner_blocks
        away_keys = mid_in[:, 0, pair].reshape(away, PAIR)
        for side in range(2):
            head = 2 * pair + side
            own = head % seg_count
            start = own * mid + part * block
            target = pl.ds(pl.multiple_of(start, block), block)
            total, highest = attend(
                qm[head, target], [kp[pair], away_keys], [vb[head], vmid[head]]
            )
            outp[pair, target, lanes(side)] = divide(total)[:, lanes(side)]
            kept = pl.ds(pl.multiple_of(part * block, block), block)
            acc_s[head, kept] = total
            max_s[head, kept] = jnp.broadcast_to(highest, (block, PAIR))
        return carry

    early = (pairs - 1) * inner_blocks
    lax.fori_loop(0, early, inner, 0)

    for copy in far_copies:
        copy.wait()
    fwd_copies = []
    for step in range(1, seg_count):
        peer = lax.rem(seg + step, seg_count)
        copy = pltpu.make_async_remote_copy(
            src_ref=far.at[seg],
            dst_ref=far.at[seg],
            send_sem=fwd_send.at[step - 1],
            recv_sem=fwd_recv.at[seg_count - 1 - step],
            device_id=(grp, peer),
            device_id_type=MESH,
        )
        copy.start()
        fwd_copies.append(copy)
    lax.fori_loop(early, pairs * inner_blocks, inner, 0)
    for copy in fwd_copies:
        copy.wait()

    far_keys_count = seg_count * SLIDE_GRP * far_pad
    wide_left = left_of(far_keys_count)
    for pair in range(pairs):
        far_keys = far[:, :, 0, pair].reshape(far_keys_count, PAIR)
        far_values = far[:, :, 1, pair].reshape(far_keys_count, PAIR).astype(F32)
        for side in range(2):
            head = 2 * pair + side
            query = q32[pair, pl.ds(head % period, far_rows, stride=period), :]
            query = jnp.where(far_left == (side == 0), query, 0.0)
            if far_pad > far_rows:
                query = jnp.concatenate([query] * (far_pad // far_rows), axis=0)
            value = jnp.where(wide_left == (side == 0), far_values, 1.0)
            if far_pad > far_rows:
                within = lax.broadcasted_iota(jnp.int32, (far_keys_count, PAIR), 0) % far_pad
                value = jnp.where(within < far_rows, value, 0.0)
            total, highest = attend(query.astype(BF16), [far_keys], [value.astype(BF16)])
            total, highest = total[:far_rows], highest[:far_rows]
            ours = pl.ds(head // seg_count % SLIDE_GRP, far_rows, stride=SLIDE_GRP)
            near_total, near_highest = acc_s[head, ours, :], max_s[head, ours, :]
            ceiling = jnp.maximum(near_highest, highest)
            joined = near_total * jnp.exp(near_highest - ceiling) + total * jnp.exp(
                highest - ceiling
            )
            place_rows = pl.ds(
                head % seg_count * mid + head // seg_count % SLIDE_GRP, far_rows, stride=SLIDE_GRP
            )
            outp[pair, place_rows, :] = jnp.where(
                far_left == (side == 0), divide(joined), outp[pair, place_rows, :]
            )

    for pair in range(pairs):
        columns = slice(pair * PAIR, (pair + 1) * PAIR)
        for residue in range(seg_count):
            k32[pair, pl.ds(residue, mid, stride=seg_count), :] = outp[
                pair, pl.ds(residue * mid, mid)
            ]
        o_ref[:, columns] = k32[pair].astype(BF16)


def body(queries, keys, values):
    rows, features = queries.shape
    seg_count = lax.axis_size("seg")
    pairs = features // PAIR
    heads = features // HEAD_WIDTH
    mid = rows // seg_count
    far_rows = rows // (SLIDE_GRP * seg_count)
    far_pad = max(16, far_rows)
    away = (seg_count - 1) * mid
    vmem = pl.BlockSpec(memory_space=pltpu.VMEM)
    dma = pltpu.SemaphoreType.DMA
    return pl.pallas_call(
        functools.partial(kernel, seg_count),
        out_shape=jax.ShapeDtypeStruct(queries.shape, BF16),
        in_specs=[vmem] * 3,
        out_specs=vmem,
        scratch_shapes=[
            pltpu.VMEM((pairs, rows, PAIR), F32),
            pltpu.VMEM((pairs, rows, PAIR), F32),
            pltpu.VMEM((pairs, rows, PAIR), F32),
            pltpu.VMEM((heads, rows, PAIR), BF16),
            pltpu.VMEM((pairs, rows, PAIR), BF16),
            pltpu.VMEM((heads, rows, PAIR), BF16),
            pltpu.VMEM((heads, rows, PAIR), BF16),
            pltpu.VMEM((2, pairs, mid, PAIR), BF16),
            pltpu.VMEM((seg_count - 1, 2, pairs, mid, PAIR), BF16),
            pltpu.VMEM((heads, away, PAIR), BF16),
            pltpu.VMEM((seg_count, SLIDE_GRP, 2, pairs, far_pad, PAIR), BF16),
            pltpu.VMEM((pairs, rows, PAIR), F32),
            pltpu.VMEM((heads, mid, PAIR), F32),
            pltpu.VMEM((heads, mid, PAIR), F32),
            dma((seg_count - 1,)),
            dma((seg_count - 1,)),
            dma((SLIDE_GRP - 1,)),
            dma((SLIDE_GRP - 1,)),
            dma((seg_count - 1,)),
            dma((seg_count - 1,)),
        ],
        compiler_params=pltpu.CompilerParams(
            collective_id=0, has_side_effects=True, vmem_limit_bytes=56 * 1024 * 1024
        ),
        name="dilated_attention",
    )(queries, keys, values)


def solution(mesh):
    spec = P(("grp", "seg"), None)
    return jax.shard_map(
        body, mesh=mesh, in_specs=(spec, spec, spec), out_specs=spec, check_vma=False
    )
```

time: 192 us -> 32.6 us (0.17)
  the two profiles are of different devices: /device:TPU:0 before, /device:TPU:13 now
where the time goes in v1:
time: 32.6 us; the launch traced here: 31.9 us
  Pallas kernels  29.8 us (91%)
  local copies, waits for them, and re-layouts  2.09 us (6%)
    pallas_call x1, Pallas kernels, body(): pl.pallas_call(functools.partial(kernel, seg_count), out_shape=jax.ShapeD...  29.8 us
    unnamed x1, local copies, waits for them, and re-layouts  2.09 us

profile of v1, /device:TPU:13, one launch (start us, length us, event | category | flops | bytes accessed | tf_op | source)
XLA Modules:
  0.0 31.9 jit_solution(9043045572451201606)
XLA Ops:
  0.0 29.8 %dilated_attention.1 = bf16[1024,384]{1,0:T(8,128)(2,1)} custom-call(bf16[1024,384]{1,0:T(8,128)(2,1)} %q_ref.1, bf16[1024,384]{1,0:T(8,128)(2,1)} %k_ref.1, bf16[1024,384]{1,0:T(8,128)(2,1)} %v_ref.1), custom_call_target="tpu_custom_call" | custom-call | tf_op jit(solution)/shard_map/dilated_attention/pallas_call | solution.py:268
  29.8 2.1 %copy.5 = bf16[1024,384]{1,0:T(8,128)(2,1)} copy(bf16[1024,384]{1,0:T(8,128)(2,1)} %dilated_attention.1) | data formatting | bytes 1572864

commit v2 on v1

--- a/solution.py
+++ b/solution.py
@@ -10,6 +10,8 @@
 HEAD_WIDTH = 64
 PAIR = 2 * HEAD_WIDTH
 SLIDE_GRP = 16
+LINE = 4
+PLANE = SLIDE_GRP // LINE
 BLOCK = 256
 
 MESH = pl.DeviceIdType.MESH
@@ -21,17 +23,27 @@
     return lax.dot_general(query, key, (((1,), (1,)), ((), ())), preferred_element_type=F32)
 
 
-def attend(query, keys, values):
-    scores = [scores_of(query, key) for key in keys]
-    highest = functools.reduce(
-        jnp.maximum, [jnp.max(one, axis=-1, keepdims=True) for one in scores]
-    )
-    total = None
-    for one, value in zip(scores, values):
-        raised = jnp.exp(one - highest).astype(BF16)
-        part = jnp.dot(raised, value, preferred_element_type=F32)
-        total = part if total is None else total + part
-    return total, highest
+def attend(jobs):
+    def scores(job):
+        query, keys, _ = job
+        return [scores_of(query, key) for key in keys]
+
+    results = []
+    ahead = scores(jobs[0])
+    for index, (_, _, values) in enumerate(jobs):
+        now = ahead
+        if index + 1 < len(jobs):
+            ahead = scores(jobs[index + 1])
+        highest = functools.reduce(
+            jnp.maximum, [jnp.max(one, axis=-1, keepdims=True) for one in now]
+        )
+        total = None
+        for one, value in zip(now, values):
+            raised = jnp.exp(one - highest).astype(BF16)
+            part = jnp.dot(raised, value, preferred_element_type=F32)
+            total = part if total is None else total + part
+        results.append((total, highest))
+    return results
 
 
 def divide(total):
@@ -42,22 +54,28 @@
     seg_count,
     q_ref, k_ref, v_ref, o_ref,
     q32, k32, v32, qm, kp, va, vb, mid_out, mid_in, vmid, far, outp, acc_s, max_s,
-    mid_send, mid_recv, far_send, far_recv, fwd_send, fwd_recv,
+    mid_send, mid_recv, line_send, line_recv, plane_send, plane_recv, fwd_send, fwd_recv,
 ):
     rows = q_ref.shape[0]
     pairs = q_ref.shape[1] // PAIR
     mid = rows // seg_count
     period = SLIDE_GRP * seg_count
     far_rows = rows // period
-    far_pad = far.shape[4]
+    far_pad = far.shape[5]
     block = min(BLOCK, mid)
     grp, seg = lax.axis_index("grp"), lax.axis_index("seg")
     place = lax.rem(grp, SLIDE_GRP)
     base = grp - place
+    line, plane = place // PLANE, lax.rem(place, PLANE)
 
     barrier = pltpu.get_barrier_semaphore()
-    for step in range(1, SLIDE_GRP):
-        peer = base + lax.rem(place + step, SLIDE_GRP)
+    line_peers = [
+        base + lax.rem(line + step, LINE) * PLANE + plane for step in range(1, LINE)
+    ]
+    plane_peers = [
+        base + line * PLANE + lax.rem(plane + step, PLANE) for step in range(1, PLANE)
+    ]
+    for peer in line_peers + plane_peers:
         pl.semaphore_signal(barrier, inc=1, device_id=(peer, seg), device_id_type=MESH)
     for step in range(1, seg_count):
         peer = lax.rem(seg + step, seg_count)
@@ -94,10 +112,10 @@
             v32[pair, pl.ds(even, mid, stride=seg_count), :],
             v32[pair, pl.ds(odd, mid, stride=seg_count), :],
         ).astype(BF16)
-        far[seg, place, 0, pair] = far_slot(k32, pair)
-        far[seg, place, 1, pair] = far_slot(v32, pair)
-
-    pl.semaphore_wait(barrier, SLIDE_GRP - 1 + seg_count - 1)
+        far[seg, plane, line, 0, pair] = far_slot(k32, pair)
+        far[seg, plane, line, 1, pair] = far_slot(v32, pair)
+
+    pl.semaphore_wait(barrier, LINE - 1 + PLANE - 1 + seg_count - 1)
 
     mid_copies = []
     for step in range(1, seg_count):
@@ -112,19 +130,18 @@
         )
         copy.start()
         mid_copies.append(copy)
-    far_copies = []
-    for step in range(1, SLIDE_GRP):
-        peer = base + lax.rem(place + step, SLIDE_GRP)
+    line_copies = []
+    for step, peer in enumerate(line_peers):
         copy = pltpu.make_async_remote_copy(
-            src_ref=far.at[seg, place],
-            dst_ref=far.at[seg, place],
-            send_sem=far_send.at[step - 1],
-            recv_sem=far_recv.at[SLIDE_GRP - 1 - step],
+            src_ref=far.at[seg, plane, line],
+            dst_ref=far.at[seg, plane, line],
+            send_sem=line_send.at[step],
+            recv_sem=line_recv.at[LINE - 2 - step],
             device_id=(peer, seg),
             device_id_type=MESH,
         )
         copy.start()
-        far_copies.append(copy)
+        line_copies.append(copy)
 
     for pair in range(pairs):
         columns = slice(pair * PAIR, (pair + 1) * PAIR)
@@ -149,20 +166,42 @@
         return slice(side * HEAD_WIDTH, (side + 1) * HEAD_WIDTH)
 
     outer_blocks = (rows - mid) // block
+    together = 2 if outer_blocks % 2 == 0 else 1
 
     def outer(index, carry):
-        pair = index // outer_blocks
-        part = index % outer_blocks
-        for side in range(2):
-            head = 2 * pair + side
-            own = head % seg_count
-            start = ((own + 1) * mid + part * block) % rows
-            target = pl.ds(pl.multiple_of(start, block), block)
-            total, _ = attend(qm[head, target], [kp[pair]], [va[head]])
+        pair = index // (outer_blocks // together)
+        first = index % (outer_blocks // together) * together
+        jobs, targets = [], []
+        for ahead in range(together):
+            for side in range(2):
+                head = 2 * pair + side
+                own = head % seg_count
+                start = ((own + 1) * mid + (first + ahead) * block) % rows
+                target = pl.ds(pl.multiple_of(start, block), block)
+                jobs.append((qm[head, target], [kp[pair]], [va[head]]))
+                targets.append((target, side))
+        for (target, side), (total, _) in zip(targets, attend(jobs)):
             outp[pair, target, lanes(side)] = divide(total)[:, lanes(side)]
         return carry
 
-    lax.fori_loop(0, pairs * outer_blocks, outer, 0)
+    outer_steps = outer_blocks // together
+    lax.fori_loop(0, outer_steps, outer, 0)
+
+    for copy in line_copies:
+        copy.wait()
+    plane_copies = []
+    for step, peer in enumerate(plane_peers):
+        copy = pltpu.make_async_remote_copy(
+            src_ref=far.at[seg, plane],
+            dst_ref=far.at[seg, plane],
+            send_sem=plane_send.at[step],
+            recv_sem=plane_recv.at[PLANE - 2 - step],
+            device_id=(peer, seg),
+            device_id_type=MESH,
+        )
+        copy.start()
+        plane_copies.append(copy)
+    lax.fori_loop(outer_steps, pairs * outer_steps, outer, 0)
 
     for copy in mid_copies:
         copy.wait()
@@ -179,16 +218,16 @@
         pair = index // inner_blocks
         part = index % inner_blocks
         away_keys = mid_in[:, 0, pair].reshape(away, PAIR)
+        kept = pl.ds(pl.multiple_of(part * block, block), block)
+        jobs, targets = [], []
         for side in range(2):
             head = 2 * pair + side
-            own = head % seg_count
-            start = own * mid + part * block
+            start = head % seg_count * mid + part * block
             target = pl.ds(pl.multiple_of(start, block), block)
-            total, highest = attend(
-                qm[head, target], [kp[pair], away_keys], [vb[head], vmid[head]]
-            )
+            jobs.append((qm[head, target], [kp[pair], away_keys], [vb[head], vmid[head]]))
+            targets.append((head, target, side))
+        for (head, target, side), (total, highest) in zip(targets, attend(jobs)):
             outp[pair, target, lanes(side)] = divide(total)[:, lanes(side)]
-            kept = pl.ds(pl.multiple_of(part * block, block), block)
             acc_s[head, kept] = total
             max_s[head, kept] = jnp.broadcast_to(highest, (block, PAIR))
         return carry
@@ -196,7 +235,7 @@
     early = (pairs - 1) * inner_blocks
     lax.fori_loop(0, early, inner, 0)
 
-    for copy in far_copies:
+    for copy in plane_copies:
         copy.wait()
     fwd_copies = []
     for step in range(1, seg_count):
@@ -218,8 +257,8 @@
     far_keys_count = seg_count * SLIDE_GRP * far_pad
     wide_left = left_of(far_keys_count)
     for pair in range(pairs):
-        far_keys = far[:, :, 0, pair].reshape(far_keys_count, PAIR)
-        far_values = far[:, :, 1, pair].reshape(far_keys_count, PAIR).astype(F32)
+        far_keys = far[:, :, :, 0, pair].reshape(far_keys_count, PAIR)
+        far_values = far[:, :, :, 1, pair].reshape(far_keys_count, PAIR).astype(F32)
         for side in range(2):
             head = 2 * pair + side
             query = q32[pair, pl.ds(head % period, far_rows, stride=period), :]
@@ -230,7 +269,7 @@
             if far_pad > far_rows:
                 within = lax.broadcasted_iota(jnp.int32, (far_keys_count, PAIR), 0) % far_pad
                 value = jnp.where(within < far_rows, value, 0.0)
-            total, highest = attend(query.astype(BF16), [far_keys], [value.astype(BF16)])
+            (total, highest), = attend([(query.astype(BF16), [far_keys], [value.astype(BF16)])])
             total, highest = total[:far_rows], highest[:far_rows]
             ours = pl.ds(head // seg_count % SLIDE_GRP, far_rows, stride=SLIDE_GRP)
             near_total, near_highest = acc_s[head, ours, :], max_s[head, ours, :]
@@ -245,13 +284,18 @@
                 far_left == (side == 0), divide(joined), outp[pair, place_rows, :]
             )
 
-    for pair in range(pairs):
-        columns = slice(pair * PAIR, (pair + 1) * PAIR)
+    o_ref[...] = outp[...].astype(BF16)
+
+
+def unsort(seg_count, sorted_ref, o_ref, stage):
+    pairs, rows, _ = sorted_ref.shape
+    mid = rows // seg_count
+    for pair in range(pairs):
         for residue in range(seg_count):
-            k32[pair, pl.ds(residue, mid, stride=seg_count), :] = outp[
+            stage[pair, pl.ds(residue, mid, stride=seg_count), :] = sorted_ref[
                 pair, pl.ds(residue * mid, mid)
-            ]
-        o_ref[:, columns] = k32[pair].astype(BF16)
+            ].astype(F32)
+        o_ref[:, pair * PAIR : (pair + 1) * PAIR] = stage[pair].astype(BF16)
 
 
 def body(queries, keys, values):
@@ -265,9 +309,9 @@
     away = (seg_count - 1) * mid
     vmem = pl.BlockSpec(memory_space=pltpu.VMEM)
     dma = pltpu.SemaphoreType.DMA
-    return pl.pallas_call(
+    ordered = pl.pallas_call(
         functools.partial(kernel, seg_count),
-        out_shape=jax.ShapeDtypeStruct(queries.shape, BF16),
+        out_shape=jax.ShapeDtypeStruct((pairs, rows, PAIR), BF16),
         in_specs=[vmem] * 3,
         out_specs=vmem,
         scratch_shapes=[
@@ -281,14 +325,16 @@
             pltpu.VMEM((2, pairs, mid, PAIR), BF16),
             pltpu.VMEM((seg_count - 1, 2, pairs, mid, PAIR), BF16),
             pltpu.VMEM((heads, away, PAIR), BF16),
-            pltpu.VMEM((seg_count, SLIDE_GRP, 2, pairs, far_pad, PAIR), BF16),
+            pltpu.VMEM((seg_count, PLANE, LINE, 2, pairs, far_pad, PAIR), BF16),
             pltpu.VMEM((pairs, rows, PAIR), F32),
             pltpu.VMEM((heads, mid, PAIR), F32),
             pltpu.VMEM((heads, mid, PAIR), F32),
             dma((seg_count - 1,)),
             dma((seg_count - 1,)),
-            dma((SLIDE_GRP - 1,)),
-            dma((SLIDE_GRP - 1,)),
+            dma((LINE - 1,)),
+            dma((LINE - 1,)),
+            dma((PLANE - 1,)),
+            dma((PLANE - 1,)),
             dma((seg_count - 1,)),
             dma((seg_count - 1,)),
         ],
@@ -297,6 +343,15 @@
         ),
         name="dilated_attention",
     )(queries, keys, values)
+    return pl.pallas_call(
+        functools.partial(unsort, seg_count),
+        out_shape=jax.ShapeDtypeStruct(queries.shape, BF16),
+        in_specs=[vmem],
+        out_specs=vmem,
+        scratch_shapes=[pltpu.VMEM((pairs, rows, PAIR), F32)],
+        compiler_params=pltpu.CompilerParams(vmem_limit_bytes=32 * 1024 * 1024),
+        name="token_order",
+    )(ordered)
 
 
 def solution(mesh):

time: 32.6 us -> 28 us (0.86); the launches traced: 31.9 us -> 27.7 us
  Pallas kernels: 29.8 us -> 26.5 us
  local copies, waits for them, and re-layouts: 2.09 us -> 1.13 us
    pallas_call x1, Pallas kernels: 29.8 us -> 25.4 us  [body(): pl.pallas_call(functools.partial(kernel, seg_count), out_shape=jax.ShapeD...]
    pallas_call x0 -> x1, Pallas kernels: none -> 1.09 us  [body(): pl.pallas_call(functools.partial(unsort, seg_count), out_shape=jax.ShapeD...]
    unnamed x1 -> x2, local copies, waits for them, and re-layouts: 2.09 us -> 1.13 us
where the time goes in v2:
time: 28 us; the launch traced here: 27.7 us
  Pallas kernels  26.5 us (95%)
  local copies, waits for them, and re-layouts  1.13 us (4%)
    pallas_call x1, Pallas kernels, body(): pl.pallas_call(functools.partial(kernel, seg_count), out_shape=jax.ShapeD...  25.4 us
    unnamed x2, local copies, waits for them, and re-layouts  1.13 us
    pallas_call x1, Pallas kernels, body(): pl.pallas_call(functools.partial(unsort, seg_count), out_shape=jax.ShapeD...  1.09 us

profile of v2, /device:TPU:13, one launch (start us, length us, event | category | flops | bytes accessed | tf_op | source)
XLA Modules:
  0.0 27.7 jit_solution(5812546227267414871)
XLA Ops:
  0.0 25.4 %dilated_attention.1.sorted_ref = bf16[3,1024,128]{2,1,0:T(8,128)(2,1)} custom-call(bf16[1024,384]{1,0:T(8,128)(2,1)} %q_ref.1, bf16[1024,384]{1,0:T(8,128)(2,1)} %k_ref.1, bf16[1024,384]{1,0:T(8,128)(2,1)} %v_ref.1), custom_call_target="tpu_custom_call" | custom-call | tf_op jit(solution)/shard_map/dilated_attention/pallas_call | solution.py:312
  25.4 0.0 copy-start
  25.5 1.1 %copy-done = bf16[3,1024,128]{2,1,0:T(8,128)(2,1)S(1)} copy-done((bf16[3,1024,128]{2,1,0:T(8,128)(2,1)S(1)}, bf16[3,1024,128]{2,1,0:T(8,128)(2,1)}, u32[]{:S(2)}) %copy-start) | copy-done | bytes 786456
  26.6 1.1 %token_order.1 = bf16[1024,384]{1,0:T(8,128)(2,1)} custom-call(bf16[3,1024,128]{2,1,0:T(8,128)(2,1)S(1)} %copy-done), custom_call_target="tpu_custom_call" | custom-call | tf_op jit(solution)/shard_map/token_order/pallas_call | solution.py:346
Async XLA Ops:
  25.4 1.1 %copy-start = (bf16[3,1024,128]{2,1,0:T(8,128)(2,1)S(1)}, bf16[3,1024,128]{2,1,0:T(8,128)(2,1)}, u32[]{:S(2)}) copy-start(bf16[3,1024,128]{2,1,0:T(8,128)(2,1)} %dilated_attention.1.sorted_ref) | copy-start | bytes 2359300

commit v3 on v2

--- a/solution.py
+++ b/solution.py
@@ -214,25 +214,23 @@
 
     inner_blocks = mid // block
 
-    def inner(index, carry):
-        pair = index // inner_blocks
-        part = index % inner_blocks
+    def inner(pair, carry):
         away_keys = mid_in[:, 0, pair].reshape(away, PAIR)
-        kept = pl.ds(pl.multiple_of(part * block, block), block)
         jobs, targets = [], []
-        for side in range(2):
-            head = 2 * pair + side
-            start = head % seg_count * mid + part * block
-            target = pl.ds(pl.multiple_of(start, block), block)
-            jobs.append((qm[head, target], [kp[pair], away_keys], [vb[head], vmid[head]]))
-            targets.append((head, target, side))
-        for (head, target, side), (total, highest) in zip(targets, attend(jobs)):
+        for part in range(inner_blocks):
+            for side in range(2):
+                head = 2 * pair + side
+                start = head % seg_count * mid + part * block
+                target = pl.ds(pl.multiple_of(start, block), block)
+                jobs.append((qm[head, target], [kp[pair], away_keys], [vb[head], vmid[head]]))
+                targets.append((head, target, side, pl.ds(part * block, block)))
+        for (head, target, side, kept), (total, highest) in zip(targets, attend(jobs)):
             outp[pair, target, lanes(side)] = divide(total)[:, lanes(side)]
             acc_s[head, kept] = total
             max_s[head, kept] = jnp.broadcast_to(highest, (block, PAIR))
         return carry
 
-    early = (pairs - 1) * inner_blocks
+    early = pairs - 1
     lax.fori_loop(0, early, inner, 0)
 
     for copy in plane_copies:
@@ -250,12 +248,13 @@
         )
         copy.start()
         fwd_copies.append(copy)
-    lax.fori_loop(early, pairs * inner_blocks, inner, 0)
+    lax.fori_loop(early, pairs, inner, 0)
     for copy in fwd_copies:
         copy.wait()
 
     far_keys_count = seg_count * SLIDE_GRP * far_pad
     wide_left = left_of(far_keys_count)
+    jobs = []
     for pair in range(pairs):
         far_keys = far[:, :, :, 0, pair].reshape(far_keys_count, PAIR)
         far_values = far[:, :, :, 1, pair].reshape(far_keys_count, PAIR).astype(F32)
@@ -269,7 +268,13 @@
             if far_pad > far_rows:
                 within = lax.broadcasted_iota(jnp.int32, (far_keys_count, PAIR), 0) % far_pad
                 value = jnp.where(within < far_rows, value, 0.0)
-            (total, highest), = attend([(query.astype(BF16), [far_keys], [value.astype(BF16)])])
+            jobs.append((query.astype(BF16), [far_keys], [value.astype(BF16)]))
+
+    results = attend(jobs)
+    for pair in range(pairs):
+        for side in range(2):
+            head = 2 * pair + side
+            total, highest = results[head]
             total, highest = total[:far_rows], highest[:far_rows]
             ours = pl.ds(head // seg_count % SLIDE_GRP, far_rows, stride=SLIDE_GRP)
             near_total, near_highest = acc_s[head, ours, :], max_s[head, ours, :]

time: 28 us -> 27.1 us (0.968)
  Pallas kernels: 26.5 us -> 25.8 us
    pallas_call x1, Pallas kernels: 25.4 us -> 24.7 us  [body(): pl.pallas_call(functools.partial(kernel, seg_count), out_shape=jax.ShapeD...]
where the time goes in v3:
time: 27.1 us; the launch traced here: 26.9 us
  Pallas kernels  25.8 us (95%)
  local copies, waits for them, and re-layouts  1.13 us (4%)
    pallas_call x1, Pallas kernels, body(): pl.pallas_call(functools.partial(kernel, seg_count), out_shape=jax.ShapeD...  24.7 us
    unnamed x2, local copies, waits for them, and re-layouts  1.13 us
    pallas_call x1, Pallas kernels, body(): pl.pallas_call(functools.partial(unsort, seg_count), out_shape=jax.ShapeD...  1.09 us

profile of v3, /device:TPU:13, one launch (start us, length us, event | category | flops | bytes accessed | tf_op | source)
XLA Modules:
  0.0 26.9 jit_solution(8870486242440249229)
XLA Ops:
  0.0 24.7 %dilated_attention.1.sorted_ref = bf16[3,1024,128]{2,1,0:T(8,128)(2,1)} custom-call(bf16[1024,384]{1,0:T(8,128)(2,1)} %q_ref.1, bf16[1024,384]{1,0:T(8,128)(2,1)} %k_ref.1, bf16[1024,384]{1,0:T(8,128)(2,1)} %v_ref.1), custom_call_target="tpu_custom_call" | custom-call | tf_op jit(solution)/shard_map/dilated_attention/pallas_call | solution.py:317
  24.7 0.0 copy-start
  24.7 1.1 %copy-done = bf16[3,1024,128]{2,1,0:T(8,128)(2,1)S(1)} copy-done((bf16[3,1024,128]{2,1,0:T(8,128)(2,1)S(1)}, bf16[3,1024,128]{2,1,0:T(8,128)(2,1)}, u32[]{:S(2)}) %copy-start) | copy-done | bytes 786456
  25.8 1.1 %token_order.1 = bf16[1024,384]{1,0:T(8,128)(2,1)} custom-call(bf16[3,1024,128]{2,1,0:T(8,128)(2,1)S(1)} %copy-done), custom_call_target="tpu_custom_call" | custom-call | tf_op jit(solution)/shard_map/token_order/pallas_call | solution.py:351
Async XLA Ops:
  24.7 1.1 %copy-start = (bf16[3,1024,128]{2,1,0:T(8,128)(2,1)S(1)}, bf16[3,1024,128]{2,1,0:T(8,128)(2,1)}, u32[]{:S(2)}) copy-start(bf16[3,1024,128]{2,1,0:T(8,128)(2,1)} %dilated_attention.1.sorted_ref) | copy-start | bytes 2359300

commit v4 on v3

--- a/solution.py
+++ b/solution.py
@@ -12,7 +12,7 @@
 SLIDE_GRP = 16
 LINE = 4
 PLANE = SLIDE_GRP // LINE
-BLOCK = 256
+BLOCK = 512
 
 MESH = pl.DeviceIdType.MESH
 F32 = jnp.float32

time: 27.1 us -> 27.1 us (level)
  no operation moved by 1% of the time
where the time goes in v4:
time: 27.1 us; the launch traced here: 26.9 us
  Pallas kernels  25.8 us (95%)
  local copies, waits for them, and re-layouts  1.13 us (4%)
    pallas_call x1, Pallas kernels, body(): pl.pallas_call(functools.partial(kernel, seg_count), out_shape=jax.ShapeD...  24.7 us
    unnamed x2, local copies, waits for them, and re-layouts  1.13 us
    pallas_call x1, Pallas kernels, body(): pl.pallas_call(functools.partial(unsort, seg_count), out_shape=jax.ShapeD...  1.09 us

profile of v4, /device:TPU:13, one launch (start us, length us, event | category | flops | bytes accessed | tf_op | source)
XLA Modules:
  0.0 26.9 jit_solution(1796694352545873348)
XLA Ops:
  0.0 24.7 %dilated_attention.1.sorted_ref = bf16[3,1024,128]{2,1,0:T(8,128)(2,1)} custom-call(bf16[1024,384]{1,0:T(8,128)(2,1)} %q_ref.1, bf16[1024,384]{1,0:T(8,128)(2,1)} %k_ref.1, bf16[1024,384]{1,0:T(8,128)(2,1)} %v_ref.1), custom_call_target="tpu_custom_call" | custom-call | tf_op jit(solution)/shard_map/dilated_attention/pallas_call | solution.py:317
  24.7 0.0 copy-start
  24.7 1.1 %copy-done = bf16[3,1024,128]{2,1,0:T(8,128)(2,1)S(1)} copy-done((bf16[3,1024,128]{2,1,0:T(8,128)(2,1)S(1)}, bf16[3,1024,128]{2,1,0:T(8,128)(2,1)}, u32[]{:S(2)}) %copy-start) | copy-done | bytes 786456
  25.8 1.1 %token_order.1 = bf16[1024,384]{1,0:T(8,128)(2,1)} custom-call(bf16[3,1024,128]{2,1,0:T(8,128)(2,1)S(1)} %copy-done), custom_call_target="tpu_custom_call" | custom-call | tf_op jit(solution)/shard_map/token_order/pallas_call | solution.py:351
Async XLA Ops:
  24.7 1.1 %copy-start = (bf16[3,1024,128]{2,1,0:T(8,128)(2,1)S(1)}, bf16[3,1024,128]{2,1,0:T(8,128)(2,1)}, u32[]{:S(2)}) copy-start(bf16[3,1024,128]{2,1,0:T(8,128)(2,1)} %dilated_attention.1.sorted_ref) | copy-start | bytes 2359300

commit v5 on v3

--- a/solution.py
+++ b/solution.py
@@ -208,9 +208,10 @@
     away = (seg_count - 1) * mid
     away_left = left_of(away)
     for pair in range(pairs):
-        value = mid_in[:, 1, pair].reshape(away, PAIR).astype(F32)
-        vmid[2 * pair] = jnp.where(away_left, value, 1.0).astype(BF16)
-        vmid[2 * pair + 1] = jnp.where(away_left, 1.0, value).astype(BF16)
+        value = mid_in[:, 1, pair].reshape(away, PAIR)
+        ones = jnp.ones_like(value)
+        vmid[2 * pair] = jnp.where(away_left, value, ones)
+        vmid[2 * pair + 1] = jnp.where(away_left, ones, value)
 
     inner_blocks = mid // block
 
@@ -257,18 +258,19 @@
     jobs = []
     for pair in range(pairs):
         far_keys = far[:, :, :, 0, pair].reshape(far_keys_count, PAIR)
-        far_values = far[:, :, :, 1, pair].reshape(far_keys_count, PAIR).astype(F32)
+        far_values = far[:, :, :, 1, pair].reshape(far_keys_count, PAIR)
         for side in range(2):
             head = 2 * pair + side
             query = q32[pair, pl.ds(head % period, far_rows, stride=period), :]
             query = jnp.where(far_left == (side == 0), query, 0.0)
             if far_pad > far_rows:
                 query = jnp.concatenate([query] * (far_pad // far_rows), axis=0)
-            value = jnp.where(wide_left == (side == 0), far_values, 1.0)
+            ones = jnp.ones_like(far_values)
+            value = jnp.where(wide_left, *((far_values, ones) if side == 0 else (ones, far_values)))
             if far_pad > far_rows:
                 within = lax.broadcasted_iota(jnp.int32, (far_keys_count, PAIR), 0) % far_pad
-                value = jnp.where(within < far_rows, value, 0.0)
-            jobs.append((query.astype(BF16), [far_keys], [value.astype(BF16)]))
+                value = jnp.where(within < far_rows, value, jnp.zeros_like(value))
+            jobs.append((query.astype(BF16), [far_keys], [value]))
 
     results = attend(jobs)
     for pair in range(pairs):

time: 27.1 us -> 27.1 us (level)
  no operation moved by 1% of the time
where the time goes in v5:
time: 27.1 us; the launch traced here: 26.9 us
  Pallas kernels  25.8 us (95%)
  local copies, waits for them, and re-layouts  1.13 us (4%)
    pallas_call x1, Pallas kernels, body(): pl.pallas_call(functools.partial(kernel, seg_count), out_shape=jax.ShapeD...  24.7 us
    unnamed x2, local copies, waits for them, and re-layouts  1.13 us
    pallas_call x1, Pallas kernels, body(): pl.pallas_call(functools.partial(unsort, seg_count), out_shape=jax.ShapeD...  1.09 us

profile of v5, /device:TPU:13, one launch (start us, length us, event | category | flops | bytes accessed | tf_op | source)
XLA Modules:
  0.0 26.9 jit_solution(3431225208675482812)
XLA Ops:
  0.0 24.7 %dilated_attention.1.sorted_ref = bf16[3,1024,128]{2,1,0:T(8,128)(2,1)} custom-call(bf16[1024,384]{1,0:T(8,128)(2,1)} %q_ref.1, bf16[1024,384]{1,0:T(8,128)(2,1)} %k_ref.1, bf16[1024,384]{1,0:T(8,128)(2,1)} %v_ref.1), custom_call_target="tpu_custom_call" | custom-call | tf_op jit(solution)/shard_map/dilated_attention/pallas_call | solution.py:319
  24.7 0.0 copy-start
  24.7 1.1 %copy-done = bf16[3,1024,128]{2,1,0:T(8,128)(2,1)S(1)} copy-done((bf16[3,1024,128]{2,1,0:T(8,128)(2,1)S(1)}, bf16[3,1024,128]{2,1,0:T(8,128)(2,1)}, u32[]{:S(2)}) %copy-start) | copy-done | bytes 786456
  25.8 1.1 %token_order.1 = bf16[1024,384]{1,0:T(8,128)(2,1)} custom-call(bf16[3,1024,128]{2,1,0:T(8,128)(2,1)S(1)} %copy-done), custom_call_target="tpu_custom_call" | custom-call | tf_op jit(solution)/shard_map/token_order/pallas_call | solution.py:353
Async XLA Ops:
  24.7 1.1 %copy-start = (bf16[3,1024,128]{2,1,0:T(8,128)(2,1)S(1)}, bf16[3,1024,128]{2,1,0:T(8,128)(2,1)}, u32[]{:S(2)}) copy-start(bf16[3,1024,128]{2,1,0:T(8,128)(2,1)} %dilated_attention.1.sorted_ref) | copy-start | bytes 2359300
